TPU v7x, 32 devices: a whole 2x2x4 slice. The times are simulated.
32 devices in a mesh: parts: 2 (over x), obs: 16 (over z, y, core).
Axes of the slice: x: 2, y: 2, z: 4, core: 2. Of those that a mesh axis runs over, the one named last changes fastest.
Arguments:
- theta: bfloat16 [1024, 24576], P(None, ('parts', 'obs')), parts along dimension 1, may hold values from -6 to 6
- predictions: bfloat16 [1024, 8192], P(None, ('parts', 'obs')), parts along dimension 1, may hold values from -6 to 6
- perturb: bfloat16 [1024, 8192], P(None, ('parts', 'obs')), parts along dimension 1, may hold values from -6 to 6
- obs_value: float32 [8192], P(('parts', 'obs')), parts along dimension 0, may hold values from -6 to 6
- obs_prec: float32 [8192], P(('parts', 'obs')), parts along dimension 0, may hold values from 0.3 to 3
- pattern: int32 [96, 8], P(('parts', 'obs')), parts along dimension 0, may hold values from 0 to 16, as said below
- obs_count: int32 [32], P('parts'), parts along dimension 0, may hold values from 64 to 256, as said below
Outputs:
- theta_new: bfloat16 [1024, 24576], P(None, ('parts', 'obs')), parts along dimension 1
There are 2 independent parts, one for each index of `parts`. A program takes and returns all parts, laid end to end along the dimension named above; each array names one. Nothing has to cross between parts.
Inputs may be any that keep to these rules, and one draw needn't show every extreme that they name: `pattern`: each row names one to 8 distinct observation blocks, the rest of its slots hold 16; some row names exactly 8. `obs_count`: some block uses all 256 slots.
All inputs are finite; a program needn't handle non-finite values.
Results may differ from a plain program's by a relative error of at most 0.0043.
Values may be sent and summed in bfloat16 or wider, within the bound.
A program may use at most 192 MiB of HBM per device.

v0:
```python
import jax
import jax.numpy as jnp
from jax import lax
from jax.sharding import PartitionSpec as P


def body(theta, predictions, perturb, obs_value, obs_prec, pattern, obs_count):
    members = theta.shape[0]
    block_width = obs_value.shape[0]
    groups = theta.shape[1] // block_width
    all_blocks = lax.axis_size("obs")
    my_index = lax.axis_index("obs")
    theta_f = theta.astype(jnp.float32)
    theta_anom = (theta_f - jnp.mean(theta_f, axis=0, keepdims=True)).astype(jnp.bfloat16)
    pred_f = predictions.astype(jnp.float32)
    pred_anom = (pred_f - jnp.mean(pred_f, axis=0, keepdims=True)).astype(jnp.bfloat16)
    usable = (jnp.arange(block_width, dtype=jnp.int32) < obs_count[my_index]).astype(jnp.float32)
    innovation = (
        usable[None, :]
        * (
            obs_prec[None, :] * (obs_value[None, :] - pred_f)
            + jnp.sqrt(obs_prec)[None, :] * perturb.astype(jnp.float32)
        )
    ).astype(jnp.bfloat16)
    linked = jnp.any(
        pattern[:, :, None] == jnp.arange(all_blocks, dtype=jnp.int32)[None, None, :], axis=1
    ).astype(jnp.float32)
    pred_piece = lax.all_gather(pred_anom, "obs", axis=1, tiled=True)
    innov_piece = lax.all_gather(innovation, "obs", axis=1, tiled=True)
    piece_blocks = pred_piece.shape[1] // block_width
    cross = jnp.dot(pred_piece.T, theta_anom, preferred_element_type=jnp.float32)
    cross = cross.reshape(piece_blocks, block_width, groups, block_width)
    cross = (cross * linked.T[:, None, :, None]).astype(jnp.bfloat16)
    cross = cross.reshape(piece_blocks * block_width, groups * block_width)
    totals = jnp.dot(innov_piece, cross, preferred_element_type=jnp.float32)
    local_misfit = jnp.sum(jnp.square(innovation.astype(jnp.float32)))
    misfit = lax.psum(local_misfit, "obs")
    obs_total = jnp.sum(obs_count).astype(jnp.float32)
    step_size = 1.0 / (1.0 + misfit / (members * obs_total))
    return (theta_f + step_size / (members - 1) * totals).astype(jnp.bfloat16)


def solution(mesh):
    return jax.shard_map(
        body,
        mesh=mesh,
        in_specs=(
            P(None, ("parts", "obs")),
            P(None, ("parts", "obs")),
            P(None, ("parts", "obs")),
            P(("parts", "obs")),
            P(("parts", "obs")),
            P(("parts", "obs"), None),
            P("parts"),
        ),
        out_specs=P(None, ("parts", "obs")),
        check_vma=False,
    )
```

profile of v0, /device:TPU:0, one launch (start us, length us, event | category | flops | bytes accessed | tf_op | source)
XLA Modules:
  0.0 206.4 jit_solution(8110599325236927020)
XLA Ops:
  6.5 0.0 all-gather.3.cloned.1.call-start
  6.5 0.7 sqrt.3
  7.2 1.2 dynamic_slice.3
  8.5 0.6 compare_convert_fusion
  9.1 1.2 convert_reduce_fusion.1
  10.3 3.3 %multiply_reduce_fusion = (f32[]{:T(128)}, bf16[1024,256]{1,0:T(8,128)(2,1)}, bf16[1024,256]{1,0:T(8,128)(2,1)}) fusion(bf16[1024,256]{1,0:T(8,128)(2,1)} %param.9, f32[256]{0:T(256)S(1)} %sqrt.3, bf16[1024,256]{1,0:T(8,128)(2,1)} %param.8, f32[256]{0:T(256)} %param.10, f32[256]{0:T(256)} %param.11, f32[256]{0:T(256)S(1)} %compare_convert_fusion, ...), kind=kLoop, calls=%fused_computation.16 | loop fusion | flops 3407871 | bytes 2102276 | tf_op jit(solution)/shard_map/reduce_sum | solution.py:36
  13.6 0.0 all-gather.3.cloned.1.call-update
  13.6 0.0 all-gather.5.cloned.1.call-start
  13.6 0.7 all-gather.5.cloned.1.call-update
  14.4 36.2 %psum.7 = f32[]{:T(128)} all-reduce(f32[]{:T(128)} %get-tuple-element.5), channel_id=1, replica_groups=mesh['parts'=2,'obs'=16] {'obs'}, use_global_device_ids=true, to_apply=%region_1.0 | all-reduce | flops 1 | bytes 8 | tf_op jit(solution)/shard_map/psum | solution.py:37
  50.5 1.4 reduce_sum.37
  51.9 0.8 fusion.12
  52.7 6.2 %mul.52 = f32[16,256,3,256]{1,0,3,2:T(8,128)} broadcast(f32[16,3]{0,1:T(4,128)S(1)} %convert_bitcast_fusion), dimensions={0,2} | broadcast | bytes 12583104 | tf_op jit(solution)/shard_map/mul | solution.py:33
  58.9 21.8 %copy.9 = f32[96,8,16,256]{3,1,2,0:T(8,128)} copy(f32[96,8,16,256]{3,2,1,0:T(8,128)} %bitcast.10) | data formatting | bytes 25165824
  80.7 0.0 copy-start
  80.7 12.7 %copy.8 = f32[4096,768]{1,0:T(8,128)} copy(f32[4096,768]{0,1:T(8,128)} %bitcast.11) | data formatting | bytes 25165824 | tf_op jit(solution)/shard_map/mul | solution.py:33
  94.8 0.0 copy-done
  94.8 0.3 convert_reduce_fusion
  95.1 0.0 all-gather.3.cloned.1.call-done
  95.1 78.3 %all-gather.5.cloned.1.call-done = bf16[1024,4096]{1,0:T(8,128)(2,1)} async-done(((bf16[1024,256]{1,0:T(8,128)(2,1)}), bf16[1024,4096]{1,0:T(8,128)(2,1)}) %all-gather.5.cloned.1.call-update) | async-done | bytes 8388624 | tf_op jit(solution)/shard_map/all_gather | solution.py:28
  173.4 26.2 %fusion.2 = bf16[1024,768]{1,0:T(8,128)(2,1)} fusion(bf16[1024,768]{1,0:T(8,128)(2,1)S(1)} %copy-done, bf16[1024,4096]{1,0:T(8,128)(2,1)} %all-gather.3.cloned.1.call-done, f32[4096,768]{1,0:T(8,128)} %copy.8, bf16[1024,4096]{1,0:T(8,128)(2,1)} %all-gather.5.cloned.1.call-done, f32[768]{0:T(1024)S(1)} %broadcast_multiply_fusion, f32[]{:T(128)S(6)} %div.23), kind=kOutput, calls=%fused_computation.6 | convolution fusion | flops 12896698368 | bytes 32508932 | tf_op jit(solution)/shard_map/dot_general | solution.py:35
  (3 shorter events, 0.0 us)
Async XLA Ops:
  6.5 88.6 %all-gather.3.cloned.1.call-start = ((), (), s32[]{:S(2)}) async-start(), calls=%async_computation | async-start | bytes 8912896 | tf_op jit(solution)/shard_map/all_gather | solution.py:29
  13.6 159.8 %all-gather.5.cloned.1.call-start = ((), (), s32[]{:S(2)}) async-start(), calls=%async_computation.1 | async-start | bytes 8912896 | tf_op jit(solution)/shard_map/all_gather | solution.py:28
  80.7 14.1 %copy-start = (bf16[1024,768]{1,0:T(8,128)(2,1)S(1)}, bf16[1024,768]{1,0:T(8,128)(2,1)}, u32[]{:S(2)}) copy-start(bf16[1024,768]{1,0:T(8,128)(2,1)} %param.7) | copy-start | bytes 4718596
Sparse Core Ops, SparseCore 0:
  13.7 80.9 all-gather.2
  96.9 76.5 all-gather.4
where the time goes:
time: 207 us; the launch traced here: 206 us
  waiting for transfers between devices  79 us (38%)
  local copies, waits for them, and re-layouts  42.7 us (21%)
  blocking collectives  36.2 us (17%)
  matrix products  26.2 us (13%)
  between operations  14.8 us (7%)
  other arithmetic  7.54 us (4%)
    all_gather x1, waiting for transfers between devices, body(): pred_piece = lax.all_gather(pred_anom, 'obs', axis=1, tiled=True)  78.3 us
    psum x1, blocking collectives, body(): misfit = lax.psum(local_misfit, 'obs')  36.2 us
    dot_general x1, matrix products, body(): totals = jnp.dot(innov_piece, cross, preferred_element_type=jnp.float32)  26.2 us
    unnamed x3, local copies, waits for them, and re-layouts  21.8 us
    mul x2, local copies, waits for them, and re-layouts, body(): cross = (cross * linked.T[:, None, :, None]).astype(jnp.bfloat16)  19 us
  transfers between devices with their start and end apart: 2, of which 1 were waited for; matrix products, arithmetic and copies ran while one was open for 21% of the time, Pallas kernels for 0%

commit v1 on v0

v1 whole, which is shorter than its diff:
```python
import functools
import jax
import jax.numpy as jnp
from jax import lax
from jax.experimental import pallas as pl
from jax.experimental.pallas import tpu as pltpu
from jax.sharding import PartitionSpec as P

MESH = pl.DeviceIdType.MESH
F32 = jnp.float32
BF16 = jnp.bfloat16
PRED_PIECES = 2
CHUNKS = 8
AHEAD = 3


def kernel(
    nz,
    theta_ref, pred_ref, pert_ref, val_ref, prec_ref, patt_ref, count_ref,
    out_ref,
    th, pall, iall, cross, own_sum, psend, precv, mask, mis,
    ps, pr, isd, ir, ts, tr, ks, kr, ms, mr, us, ur,
):
    members, width = theta_ref.shape
    blk = pred_ref.shape[1]
    groups = width // blk
    nobs = nz * 4
    rp = blk // PRED_PIECES
    rk = members // CHUNKS
    part = lax.axis_index("parts")
    me = lax.axis_index("obs")
    z = me // 4
    y = (me // 2) % 2
    c = me % 2

    def dev(zz, yy, cc):
        return (part, zz * 4 + yy * 2 + cc)

    sib = dev(z, y, 1 - c)
    mate = dev(z, 1 - y, c)

    barrier = pltpu.get_barrier_semaphore()
    pl.semaphore_signal(barrier, inc=1, device_id=sib, device_id_type=MESH)
    pl.semaphore_signal(barrier, inc=1, device_id=mate, device_id_type=MESH)
    for h in range(1, nz):
        pl.semaphore_signal(
            barrier, inc=1, device_id=dev((z + h) % nz, y, c), device_id_type=MESH
        )

    def target(d):
        return (dev(z + 1, y, c), dev(z - 1, y, c), sib)[d]

    def pcopy(zz, cc, p, d):
        r = pall.at[pl.ds(pl.multiple_of((zz * 2 + cc) * blk + p * rp, rp), rp), :]
        return pltpu.make_async_remote_copy(
            src_ref=r, dst_ref=r, send_sem=ps.at[d, p, zz], recv_sem=pr.at[p, zz * 2 + cc],
            device_id=target(d), device_id_type=MESH,
        )

    def icopy(zz, cc, k, d):
        r = iall.at[
            pl.ds(pl.multiple_of(k * rk, rk), rk),
            pl.ds(pl.multiple_of((zz * 2 + cc) * blk, blk), blk),
        ]
        return pltpu.make_async_remote_copy(
            src_ref=r, dst_ref=r, send_sem=isd.at[d, k, zz], recv_sem=ir.at[k, zz * 2 + cc],
            device_id=target(d), device_id_type=MESH,
        )

    def send_own(copy, p):
        @pl.when(z + 1 < nz)
        def _():
            copy(z, c, p, 0).start()

        @pl.when(z >= 1)
        def _():
            copy(z, c, p, 1).start()

    def relay(copy, s, p):
        below = z - 1 - s
        above = z + 1 + s

        @pl.when(below >= 0)
        def _():
            copy(below, c, p, 2).wait_recv()

            @pl.when(z + 1 < nz)
            def _():
                copy(below, c, p, 0).start()

            copy(below, c, p, 2).start()

        @pl.when(above < nz)
        def _():
            copy(above, c, p, 2).wait_recv()

            @pl.when(z >= 1)
            def _():
                copy(above, c, p, 1).start()

            copy(above, c, p, 2).start()

    def tcopy(t):
        return pltpu.make_async_remote_copy(
            src_ref=th.at[0, t], dst_ref=th.at[1, t], send_sem=ts.at[t], recv_sem=tr.at[t],
            device_id=mate, device_id_type=MESH,
        )

    kcopy = pltpu.make_async_remote_copy(
        src_ref=mask.at[0], dst_ref=mask.at[1], send_sem=ks, recv_sem=kr,
        device_id=mate, device_id_type=MESH,
    )

    def ucopy(k):
        rows = pl.ds(pl.multiple_of(k * rk, rk), rk)
        return pltpu.make_async_remote_copy(
            src_ref=psend.at[rows, :], dst_ref=precv.at[rows, :],
            send_sem=us.at[k], recv_sem=ur.at[k], device_id=mate, device_id_type=MESH,
        )

    def mcopy(src, dst, sem, device):
        return pltpu.make_async_remote_copy(
            src_ref=mis.at[src], dst_ref=mis.at[dst], send_sem=ms.at[sem], recv_sem=mr.at[dst],
            device_id=device, device_id_type=MESH,
        )

    pred_f = pred_ref[...].astype(F32)
    anom = pred_f - jnp.mean(pred_f, axis=0, keepdims=True)
    own_slot = z * 2 + c
    pall[pl.ds(pl.multiple_of(own_slot * blk, blk), blk), :] = anom.T.astype(BF16)

    pl.semaphore_wait(barrier, nz + 1)
    for p in range(PRED_PIECES):
        send_own(pcopy, p)
    for t in range(groups):
        x = theta_ref[:, t * blk:(t + 1) * blk].astype(F32)
        th[0, t] = (x - jnp.mean(x, axis=0, keepdims=True)).astype(BF16)
        tcopy(t).start()
    for p in range(PRED_PIECES):
        pcopy(z, c, p, 2).start()

    block_of_row = lax.broadcasted_iota(jnp.int32, (nobs, blk), 0)
    for t in range(groups):
        hit = jnp.zeros((nobs, blk), F32)
        for slot in range(patt_ref.shape[1]):
            hit = jnp.where(block_of_row == patt_ref[t:t + 1, slot:slot + 1], 1.0, hit)
        mask[0, :, t * blk:(t + 1) * blk] = hit
    kcopy.start()

    column = lax.broadcasted_iota(jnp.int32, (1, blk), 1)
    usable = (column < count_ref[me]).astype(F32)
    prec = prec_ref[...]
    innov = (
        usable
        * (
            prec * (val_ref[...] - pred_ref[...].astype(F32))
            + jnp.sqrt(prec) * pert_ref[...].astype(F32)
        )
    ).astype(BF16)
    iall[:, pl.ds(pl.multiple_of(own_slot * blk, blk), blk)] = innov
    for k in range(AHEAD):
        send_own(icopy, k)
    for k in range(CHUNKS):
        icopy(z, c, k, 2).start()
    squares = jnp.square(innov.astype(F32))
    mis[0] = jnp.sum(squares.reshape(members // 8, 8, blk), axis=0)
    mcopy(0, 1, 0, sib).start()

    def cross_pair(slot, which, t):
        linked = mask[which, pl.ds((slot // 2) * 4 + y * 2 + slot % 2, 1), t * blk:(t + 1) * blk]
        rows = pl.ds(pl.multiple_of(slot * blk, blk), blk)
        found = jnp.dot(pall[rows, :], th[which, t], preferred_element_type=F32)
        at = (which * groups + t) * blk
        cross[rows, at:at + blk] = (found * linked).astype(BF16)

    def cross_own(zz):
        for p in range(PRED_PIECES):
            pcopy(zz, 1 - c, p, 2).wait_recv()

        def one(cc, _):
            for t in range(groups):
                cross_pair(zz * 2 + cc, 0, t)
            return 0

        lax.fori_loop(0, 2, one, 0)

    cross_own(z)
    for s in range(nz - 1):
        for p in range(PRED_PIECES):
            relay(pcopy, s, p)

        @pl.when(z - 1 - s >= 0)
        def _():
            cross_own(z - 1 - s)

        @pl.when(z + 1 + s < nz)
        def _():
            cross_own(z + 1 + s)

        if s == 0:
            mcopy(0, 1, 0, sib).wait_recv()
            mis[2] = mis[0] + mis[1]
            mcopy(2, 3, 1, mate).start()
        if s == 1:
            mcopy(2, 3, 1, mate).wait_recv()
            mis[4 + z] = mis[2] + mis[3]
            for h in range(1, nz):
                mcopy(4 + z, 4 + z, 1 + h, dev((z + h) % nz, y, c)).start()

    kcopy.wait_recv()
    for t in range(groups):
        tcopy(t).wait_recv()

    def mate_cross(slot, _):
        for t in range(groups):
            cross_pair(slot, 1, t)
        return 0

    lax.fori_loop(0, nz * 2, mate_cross, 0)

    for h in range(1, nz):
        other = (z + h) % nz
        mcopy(4 + other, 4 + other, 1 + h, dev(other, y, c)).wait_recv()
    tile = mis[4]
    for zz in range(1, nz):
        tile = tile + mis[4 + zz]
    misfit = jnp.sum(jnp.sum(tile, axis=0, keepdims=True), axis=1, keepdims=True)
    total = count_ref[0]
    for b in range(1, nobs):
        total = total + count_ref[b]
    scale = 1.0 / (1.0 + misfit / (members * total.astype(F32))) / (members - 1)

    def finish(k):
        ucopy(k).wait_recv()
        rows = pl.ds(pl.multiple_of(k * rk, rk), rk)
        update = own_sum[rows, :] + precv[rows, :].astype(F32)
        out_ref[rows, :] = (theta_ref[rows, :].astype(F32) + scale * update).astype(BF16)

    def chunk(k, _):
        @pl.when(k + AHEAD < CHUNKS)
        def _():
            send_own(icopy, k + AHEAD)

        for s in range(nz - 1):
            relay(icopy, s, k)
        for zz in range(nz):
            icopy(zz, 1 - c, k, 2).wait_recv()
        rows = pl.ds(pl.multiple_of(k * rk, rk), rk)
        psend[rows, :] = jnp.dot(
            iall[rows, :], cross[:, width:], preferred_element_type=F32
        ).astype(BF16)
        ucopy(k).start()
        own_sum[rows, :] = jnp.dot(
            iall[rows, :], cross[:, :width], preferred_element_type=F32
        )

        @pl.when(k >= 2)
        def _():
            finish(k - 2)

        return 0

    lax.fori_loop(0, CHUNKS, chunk, 0)
    finish(CHUNKS - 2)
    finish(CHUNKS - 1)

    def drain(copy, p):
        for zz in range(nz):
            @pl.when((z + 1 < nz) & (z >= zz))
            def _():
                copy(zz, c, p, 0).wait_send()

            @pl.when((z >= 1) & (z <= zz))
            def _():
                copy(zz, c, p, 1).wait_send()

            copy(zz, c, p, 2).wait_send()

    for p in range(PRED_PIECES):
        drain(pcopy, p)

    def drain_chunk(k, _):
        drain(icopy, k)
        ucopy(k).wait_send()
        return 0

    lax.fori_loop(0, CHUNKS, drain_chunk, 0)
    for t in range(groups):
        tcopy(t).wait_send()
    kcopy.wait_send()
    mcopy(0, 1, 0, sib).wait_send()
    mcopy(2, 3, 1, mate).wait_send()
    for h in range(1, nz):
        mcopy(4 + z, 4 + z, 1 + h, dev((z + h) % nz, y, c)).wait_send()


def body(theta, predictions, perturb, obs_value, obs_prec, pattern, obs_count):
    members, width = theta.shape
    blk = predictions.shape[1]
    groups = width // blk
    nobs = lax.axis_size("obs")
    nz = nobs // 4
    row = nz * 2
    dma = pltpu.SemaphoreType.DMA
    vmem = pl.BlockSpec(memory_space=pltpu.VMEM)
    return pl.pallas_call(
        functools.partial(kernel, nz),
        out_shape=jax.ShapeDtypeStruct((members, width), BF16),
        in_specs=[vmem] * 6 + [pl.BlockSpec(memory_space=pltpu.SMEM)],
        out_specs=vmem,
        scratch_shapes=[
            pltpu.VMEM((2, groups, members, blk), BF16),
            pltpu.VMEM((row * blk, members), BF16),
            pltpu.VMEM((members, row * blk), BF16),
            pltpu.VMEM((row * blk, 2 * width), BF16),
            pltpu.VMEM((members, width), F32),
            pltpu.VMEM((members, width), BF16),
            pltpu.VMEM((members, width), BF16),
            pltpu.VMEM((2, nobs, width), F32),
            pltpu.VMEM((4 + nz, 8, blk), F32),
            dma((3, PRED_PIECES, nz)),
            dma((PRED_PIECES, row)),
            dma((3, CHUNKS, nz)),
            dma((CHUNKS, row)),
            dma((groups,)),
            dma((groups,)),
            dma(()),
            dma(()),
            dma((1 + nz,)),
            dma((4 + nz,)),
            dma((CHUNKS,)),
            dma((CHUNKS,)),
        ],
        compiler_params=pltpu.CompilerParams(
            collective_id=0, has_side_effects=True, vmem_limit_bytes=58 * 1024 * 1024
        ),
        cost_estimate=pl.CostEstimate(
            flops=4 * members * nobs * blk * width,
            bytes_accessed=2 * members * (2 * width + 2 * blk),
            transcendentals=0,
        ),
    )(
        theta, predictions, perturb,
        obs_value.reshape(1, blk), obs_prec.reshape(1, blk), pattern, obs_count,
    )


def solution(mesh):
    return jax.shard_map(
        body,
        mesh=mesh,
        in_specs=(
            P(None, ("parts", "obs")),
            P(None, ("parts", "obs")),
            P(None, ("parts", "obs")),
            P(("parts", "obs")),
            P(("parts", "obs")),
            P(("parts", "obs"), None),
            P("parts"),
        ),
        out_specs=P(None, ("parts", "obs")),
        check_vma=False,
    )
```

time: 207 us -> 114 us (0.55)
  Pallas kernels: 0 us -> 112 us
  waiting for transfers between devices: 79 us -> 0 us
  local copies, waits for them, and re-layouts: 42.7 us -> 2.65 us
  blocking collectives: 36.2 us -> 0 us
  matrix products: 26.2 us -> 0 us
  between operations: 14.8 us -> 0.01 us
  other arithmetic: 7.54 us -> 0 us
    pallas_call x0 -> x1, Pallas kernels: none -> 112 us  [body(): pl.pallas_call(functools.partial(kernel, nz), out_shape=jax.ShapeDtypeStr...]
    all_gather x2 -> x0, waiting for transfers between devices: 78.3 us -> none  [the longest x1 78.3 us: body(): pred_piece = lax.all_gather(pred_anom, 'obs', axis=1, tiled=True)]
    psum x1 -> x0, blocking collectives: 36.2 us -> none  [body(): misfit = lax.psum(local_misfit, 'obs')]
    dot_general x1 -> x0, matrix products: 26.2 us -> none  [body(): totals = jnp.dot(innov_piece, cross, preferred_element_type=jnp.float32)]
    unnamed x3 -> x1, local copies, waits for them, and re-layouts: 21.8 us -> 2.65 us
    mul x2 -> x0, local copies, waits for them, and re-layouts: 19 us -> none  [body(): cross = (cross * linked.T[:, None, :, None]).astype(jnp.bfloat16)]
    reduce_sum x4 -> x0, other arithmetic: 6.09 us -> none  [the longest x1 3.25 us: body(): local_misfit = jnp.sum(jnp.square(innovation.astype(jnp.float32)))]
  transfers between devices with their start and end apart: 2 -> 0, of which waited for: 1 -> 0; matrix products, arithmetic and copies ran while one was open for 21% -> 0% of each run, Pallas kernels for 0% -> 0%
where the time goes in v1:
time: 114 us
  Pallas kernels  112 us (98%)
  local copies, waits for them, and re-layouts  2.65 us (2%)
    pallas_call x1, Pallas kernels, body(): pl.pallas_call(functools.partial(kernel, nz), out_shape=jax.ShapeDtypeStr...  112 us
    unnamed x1, local copies, waits for them, and re-layouts  2.65 us

profile of v1, /device:TPU:0, one launch (start us, length us, event | category | flops | bytes accessed | tf_op | source)
XLA Modules:
  0.0 114.2 jit_solution(8562371246497201433)
XLA Ops:
  0.0 111.6 %shard_map.73 = bf16[1024,768]{1,0:T(8,128)(2,1)} custom-call(bf16[1024,768]{1,0:T(8,128)(2,1)} %theta_ref.1, bf16[1024,256]{1,0:T(8,128)(2,1)} %pred_ref.1, bf16[1024,256]{1,0:T(8,128)(2,1)} %pert_ref.1, f32[1,256]{1,0:T(1,128)} %bitcast.2, f32[1,256]{1,0:T(1,128)} %bitcast.3, s32[3,8]{1,0:T(4,128)} %patt_ref.1, s32[16]{0:T(128)} %count_ref.1), custom_call_target="tpu_custom_call" | custom-call | flops 12884901888 | bytes 4194304 | tf_op jit(solution)/shard_map/pallas_call | solution.py:306
  111.6 2.7 %copy.9 = bf16[1024,768]{1,0:T(8,128)(2,1)} copy(bf16[1024,768]{1,0:T(8,128)(2,1)} %shard_map.73) | data formatting | bytes 3145728

commit v2 on v1

--- a/solution.py
+++ b/solution.py
@@ -10,8 +10,8 @@
 F32 = jnp.float32
 BF16 = jnp.bfloat16
 PRED_PIECES = 2
-CHUNKS = 8
-AHEAD = 3
+CHUNKS = 4
+AHEAD = 2
 
 
 def kernel(

time: 114 us -> 105 us (0.921)
  Pallas kernels: 112 us -> 102 us
    pallas_call x1, Pallas kernels: 112 us -> 102 us  [body(): pl.pallas_call(functools.partial(kernel, nz), out_shape=jax.ShapeDtypeStr...]
where the time goes in v2:
time: 105 us
  Pallas kernels  102 us (97%)
  local copies, waits for them, and re-layouts  2.65 us (3%)
    pallas_call x1, Pallas kernels, body(): pl.pallas_call(functools.partial(kernel, nz), out_shape=jax.ShapeDtypeStr...  102 us
    unnamed x1, local copies, waits for them, and re-layouts  2.65 us

profile of v2, /device:TPU:0, one launch (start us, length us, event | category | flops | bytes accessed | tf_op | source)
XLA Modules:
  0.0 104.7 jit_solution(8461346557205142858)
XLA Ops:
  0.0 102.1 %shard_map.73 = bf16[1024,768]{1,0:T(8,128)(2,1)} custom-call(bf16[1024,768]{1,0:T(8,128)(2,1)} %theta_ref.1, bf16[1024,256]{1,0:T(8,128)(2,1)} %pred_ref.1, bf16[1024,256]{1,0:T(8,128)(2,1)} %pert_ref.1, f32[1,256]{1,0:T(1,128)} %bitcast.2, f32[1,256]{1,0:T(1,128)} %bitcast.3, s32[3,8]{1,0:T(4,128)} %patt_ref.1, s32[16]{0:T(128)} %count_ref.1), custom_call_target="tpu_custom_call" | custom-call | flops 12884901888 | bytes 4194304 | tf_op jit(solution)/shard_map/pallas_call | solution.py:306
  102.1 2.7 %copy.9 = bf16[1024,768]{1,0:T(8,128)(2,1)} copy(bf16[1024,768]{1,0:T(8,128)(2,1)} %shard_map.73) | data formatting | bytes 3145728

commit v3 on v2

--- a/solution.py
+++ b/solution.py
@@ -207,6 +207,7 @@
             for h in range(1, nz):
                 mcopy(4 + z, 4 + z, 1 + h, dev((z + h) % nz, y, c)).start()
 
+    relay(icopy, 0, 0)
     kcopy.wait_recv()
     for t in range(groups):
         tcopy(t).wait_recv()
@@ -241,8 +242,13 @@
         def _():
             send_own(icopy, k + AHEAD)
 
-        for s in range(nz - 1):
+        for s in range(1, nz - 1):
             relay(icopy, s, k)
+
+        @pl.when(k + 1 < CHUNKS)
+        def _():
+            relay(icopy, 0, k + 1)
+
         for zz in range(nz):
             icopy(zz, 1 - c, k, 2).wait_recv()
         rows = pl.ds(pl.multiple_of(k * rk, rk), rk)

time: 105 us -> 100 us (0.952)
  Pallas kernels: 102 us -> 97.4 us
    pallas_call x1, Pallas kernels: 102 us -> 97.4 us  [body(): pl.pallas_call(functools.partial(kernel, nz), out_shape=jax.ShapeDtypeStr...]
where the time goes in v3:
time: 100 us
  Pallas kernels  97.4 us (97%)
  local copies, waits for them, and re-layouts  2.65 us (3%)
    pallas_call x1, Pallas kernels, body(): pl.pallas_call(functools.partial(kernel, nz), out_shape=jax.ShapeDtypeStr...  97.4 us
    unnamed x1, local copies, waits for them, and re-layouts  2.65 us

profile of v3, /device:TPU:0, one launch (start us, length us, event | category | flops | bytes accessed | tf_op | source)
XLA Modules:
  0.0 100.0 jit_solution(4433832882518939860)
XLA Ops:
  0.0 97.4 %shard_map.73 = bf16[1024,768]{1,0:T(8,128)(2,1)} custom-call(bf16[1024,768]{1,0:T(8,128)(2,1)} %theta_ref.1, bf16[1024,256]{1,0:T(8,128)(2,1)} %pred_ref.1, bf16[1024,256]{1,0:T(8,128)(2,1)} %pert_ref.1, f32[1,256]{1,0:T(1,128)} %bitcast.2, f32[1,256]{1,0:T(1,128)} %bitcast.3, s32[3,8]{1,0:T(4,128)} %patt_ref.1, s32[16]{0:T(128)} %count_ref.1), custom_call_target="tpu_custom_call" | custom-call | flops 12884901888 | bytes 4194304 | tf_op jit(solution)/shard_map/pallas_call | solution.py:312
  97.4 2.7 %copy.9 = bf16[1024,768]{1,0:T(8,128)(2,1)} copy(bf16[1024,768]{1,0:T(8,128)(2,1)} %shard_map.73) | data formatting | bytes 3145728
